TPU v7x, 512 devices: a whole 4x4x16 slice. The times are simulated.
512 devices in a mesh: tile: 32 (over x, z_hi, core), dir: 16 (over y, z_lo).
Axes of the slice: x: 4, y: 4, z: 16 (z_hi: 4, z_lo: 4; z = z_hi * 4 + z_lo), core: 2. Of those that a mesh axis runs over, the one named last changes fastest.
Arguments:
- background_prev: float32 [64, 256, 128], P(None, 'tile'), may hold values from -6 to 6
- background_now: float32 [64, 256, 128], P(None, 'tile'), may hold values from -6 to 6
- stiffness: bfloat16 [64, 256, 128], P(None, 'tile'), may hold values from 0.039794922 to 0.19921875
- drift_terms: bfloat16 [3, 64, 256, 128], P(None, None, 'tile'), may hold values from -0.079589844 to 0.079589844
- born_prev: bfloat16 [64, 64, 256, 128], P('dir', None, 'tile'), may hold values from -6 to 6
- born_now: bfloat16 [64, 64, 256, 128], P('dir', None, 'tile'), may hold values from -6 to 6
- pieces: bfloat16 [64, 1024, 32, 128], P('dir', 'tile'), may hold values from -6 to 6
- piece_target: int32 [1024, 1], P('tile'), may hold values from 0 to 31; in each aligned block of 32 rows (0 to 31, 32 to 63, ...) at most 2 rows name the same one
- piece_block: int32 [1024], P('tile'), may hold values from 0 to 15
- wavelet: float32 [4], replicated, may hold values from -24 to 24
- source_cell: int32 [3], replicated, may hold values from 0 to 63
- receiver_z: int32 [256], replicated, may hold values from 0 to 63
- receiver_x: int32 [256], replicated, may hold values from 0 to 255
- receiver_y: int32 [256], replicated, may hold values from 0 to 127
Outputs:
- born_field: float32 [64, 64, 256, 128], P('dir', None, 'tile')
- traces: float32 [64, 4, 256], P('dir')
Inputs may be any that keep to these rules, and one draw needn't show every extreme that they name: `piece_target`: in each aligned block of 32 rows (the rows of one device) no tile is named by more than 2 rows; in some blocks a tile is named by exactly 2 rows.
All inputs are finite; a program needn't handle non-finite values.
Results may differ from a plain program's by a relative error of at most 0.0005.
Values may be sent and summed in bfloat16 or wider, within the bound.
No kernel may reach another device: no remote copies, remote signals or barrier semaphores. Data moves between devices by JAX's collectives and lax.ppermute only.
A program may use at most 128 MiB of HBM per device.

v0:
```python
import jax
import jax.numpy as jnp
from jax import lax
from jax.sharding import PartitionSpec as P

CX = 8
ITERS = 4
ZPARTS = 2
CAP = 2
SECOND_TAPS = (-205.0 / 72.0, 8.0 / 5.0, -1.0 / 5.0, 8.0 / 315.0, -1.0 / 560.0)
FIRST_TAPS = (0.0, 4.0 / 5.0, -1.0 / 5.0, 4.0 / 105.0, -1.0 / 280.0)


def padded_2(block, sides, width):
    for axis, dim in sides:
        count = lax.axis_size(axis)
        forward = [(i, i + 1) for i in range(count - 1)]
        backward = [(target, source) for source, target in forward]
        low = lax.ppermute(
            lax.slice_in_dim(block, block.shape[dim] - width, None, axis=dim), axis, forward
        )
        high = lax.ppermute(lax.slice_in_dim(block, 0, width, axis=dim), axis, backward)
        block = jnp.concatenate([low, block, high], axis=dim)
    return block


def shifted(padded, interior, spatial, offset):
    starts = [4, 4, 4]
    starts[spatial] = 4 + offset
    leading = padded.ndim - 3
    window = tuple(
        [slice(None)] * leading
        + [slice(starts[which], starts[which] + interior[which]) for which in range(3)]
    )
    return padded[window]


def operate(padded, stiff_wide, drift_wide):
    interior = stiff_wide.shape
    center = shifted(padded, interior, 0, 0)
    second = 3.0 * SECOND_TAPS[0] * center
    slopes = jnp.zeros_like(center)
    for spatial in range(3):
        gradient = jnp.zeros_like(center)
        for offset in range(1, 5):
            forward = shifted(padded, interior, spatial, offset)
            backward = shifted(padded, interior, spatial, -offset)
            second = second + SECOND_TAPS[offset] * (forward + backward)
            gradient = gradient + FIRST_TAPS[offset] * (forward - backward)
        slopes = slopes + drift_wide[spatial] * gradient
    return stiff_wide * second + slopes


def faces(born_present, background_part):
    return (padded_2(born_present, (("tile", 2),), 4), padded_2(background_part, (("tile", 2),), 4))


def assemble(pieces, piece_target, piece_block, tile_count):
    targets = piece_target[:, 0]
    row_count = targets.shape[0]
    positions = jnp.arange(row_count)
    before = (targets[:, None] == targets[None, :]) & (positions[None, :] < positions[:, None])
    arrival = jnp.sum(before.astype(jnp.int32), axis=1)
    slot_ids = targets * CAP + arrival
    placing = (slot_ids[:, None] == jnp.arange(tile_count * CAP)[None, :]).astype(jnp.bfloat16)
    outgoing = jnp.einsum(
        "krzy,rs->kszy", pieces, placing, preferred_element_type=jnp.float32
    ).astype(jnp.bfloat16)
    labels = jnp.dot(
        (piece_block + 1).astype(jnp.bfloat16)[None, :], placing, preferred_element_type=jnp.float32
    ).astype(jnp.bfloat16)
    incoming, arrived = (
        lax.all_to_all(outgoing, "tile", split_axis=1, concat_axis=1, tiled=True),
        lax.all_to_all(labels, "tile", split_axis=1, concat_axis=1, tiled=True),
    )
    wanted = (jnp.arange(ZPARTS * CX) + 1).astype(jnp.float32)
    picking = (
        (arrived[0][:, None].astype(jnp.float32) == wanted[None, :])
        .astype(jnp.bfloat16)
        .reshape(-1, ZPARTS, CX)
    )
    perturb = jnp.einsum("kszy,spx->kpzxy", incoming, picking, preferred_element_type=jnp.float32)
    return perturb.reshape(pieces.shape[0], ZPARTS * pieces.shape[2], CX, pieces.shape[3])


def local(
    background_prev,
    background_now,
    stiffness,
    drift_terms,
    born_prev,
    born_now,
    pieces,
    piece_target,
    piece_block,
    wavelet,
    source_cell,
    receiver_z,
    receiver_x,
    receiver_y,
):
    tile_count = lax.axis_size("tile")
    tile_place = lax.axis_index("tile")
    depth_cells, width_cells, height_cells = background_now.shape
    stiff_wide = stiffness.astype(jnp.float32)
    drift_wide = drift_terms.astype(jnp.float32)
    perturb = assemble(pieces, piece_target, piece_block, tile_count)
    across_axis = (tile_place * width_cells + jnp.arange(width_cells))[None, :, None]
    height_axis = jnp.arange(height_cells)[None, None, :]
    earlier_born = born_prev.astype(jnp.float32)
    current_born = born_now.astype(jnp.float32)
    local_x = receiver_x - tile_place * width_cells
    inside = ((local_x >= 0) & (local_x < width_cells)).astype(jnp.float32)
    flat_index = (
        receiver_z * width_cells + jnp.clip(local_x, 0, width_cells - 1)
    ) * height_cells + receiver_y
    slab_cells = depth_cells // lax.axis_size("dir")
    slab_start = lax.axis_index("dir") * slab_cells
    previous = lax.dynamic_slice_in_dim(background_prev, slab_start, slab_cells, 0)
    present = lax.dynamic_slice_in_dim(background_now, slab_start, slab_cells, 0)
    slab_stiff = lax.dynamic_slice_in_dim(stiff_wide, slab_start, slab_cells, 0)
    slab_drift = lax.dynamic_slice_in_dim(drift_wide, slab_start, slab_cells, 1)
    depth_axis = (slab_start + jnp.arange(slab_cells))[:, None, None]
    source_mask = (
        (depth_axis == source_cell[0])
        & (across_axis == source_cell[1])
        & (height_axis == source_cell[2])
    ).astype(jnp.float32)
    records = []
    for step_index in range(ITERS):
        deeper = padded_2(present[None], (("dir", 1),), 4)
        born_wide, back_wide = faces(current_born, deeper)
        local_accel = operate(
            jnp.pad(back_wide[0], ((0, 0), (0, 0), (4, 4))), slab_stiff, slab_drift
        )
        acceleration = lax.all_gather(local_accel, "dir", axis=0, tiled=True)
        previous, present = (
            present,
            2.0 * present - previous + local_accel + wavelet[step_index] * source_mask,
        )
        born_padded = jnp.pad(born_wide, ((0, 0), (4, 4), (0, 0), (4, 4)))
        following = (
            2.0 * current_born
            - earlier_born
            + operate(born_padded, stiff_wide, drift_wide)
            + perturb * acceleration
        )
        records.append(
            jnp.take(following.reshape(following.shape[0], -1), flat_index, axis=1)
            * inside[None, :]
        )
        earlier_born, current_born = (current_born, following)
    traces = lax.psum(jnp.stack(records, axis=1), "tile")
    return (current_born, traces)


def solution(mesh):
    placed = (
        P(None, "tile", None),
        P(None, "tile", None),
        P(None, "tile", None),
        P(None, None, "tile", None),
        P("dir", None, "tile", None),
        P("dir", None, "tile", None),
        P("dir", "tile", None, None),
        P("tile", None),
        P("tile"),
        P(),
        P(),
        P(),
        P(),
        P(),
    )
    return jax.shard_map(
        local,
        mesh=mesh,
        in_specs=placed,
        out_specs=(P("dir", None, "tile", None), P("dir", None, None)),
        check_vma=False,
    )
```

profile of v0, /device:TPU:24, one launch (start us, length us, event | category | flops | bytes accessed | tf_op | source)
XLA Modules:
  0.0 746.2 jit_solution(9172707135732427772)
XLA Ops:
  3.8 17.9 %all-to-all-start = ((bf16[1,32,2]{2,0,1:T(2,128)(2,1)}), bf16[1,32,2]{2,0,1:T(2,128)(2,1)S(1)}, u32[]{:S(2)}, u32[]{:S(2)}) async-start(bf16[1,32,2]{2,0,1:T(2,128)(2,1)} %all_to_all.12), calls=%async_computation | async-start | bytes 32768 | tf_op jit(solution)/shard_map/all_to_all | solution.py:74
  25.4 10.8 %all-to-all-done = bf16[1,32,2]{2,0,1:T(2,128)(2,1)S(1)} async-done(((bf16[1,32,2]{2,0,1:T(2,128)(2,1)}), bf16[1,32,2]{2,0,1:T(2,128)(2,1)S(1)}, u32[]{:S(2)}, u32[]{:S(2)}) %all-to-all-start) | async-done | bytes 160 | tf_op jit(solution)/shard_map/all_to_all | solution.py:74
  36.3 4.8 all-to-all-start.1
  41.8 4.0 collective-permute-start.3
  50.1 3.8 collective-permute-start
  57.7 67.6 %collective-permute-done.3 = f32[1,4,8,128]{3,2,1,0:T(8,128)S(1)} collective-permute-done((f32[1,4,8,128]{3,2,1,0:T(8,128)S(1)}, f32[1,4,8,128]{3,2,1,0:T(8,128)S(1)}, u32[]{:S(2)}, u32[]{:S(2)}) %collective-permute-start.3) | collective-permute-done | bytes 16416 | tf_op jit(solution)/shard_map/ppermute | solution.py:22
  132.1 27.6 %collective-permute-start.9 = (f32[1,4,8,128]{3,2,1,0:T(8,128)S(1)}, f32[1,4,8,128]{3,2,1,0:T(8,128)S(1)}, u32[]{:S(2)}, u32[]{:S(2)}) collective-permute-start(f32[1,4,8,128]{3,2,1,0:T(8,128)S(1)} %bitcast.136), channel_id=1, source_target_pairs={{1,0},{2,1},{3,2},{4,3},{5,4},{6,5},{7,6},{8,7},{9,8},{10,9},{11,1... | collective-permute-start | bytes 49160 | tf_op jit(solution)/shard_map/ppermute | solution.py:22
  161.9 6.2 collective-permute-done.8
  169.4 10.4 %collective-permute-start.10 = (f32[1,12,4,128]{3,2,1,0:T(4,128)S(1)}, f32[1,12,4,128]{3,2,1,0:T(4,128)S(1)}, u32[]{:S(2)}, u32[]{:S(2)}) collective-permute-start(f32[1,12,4,128]{3,2,1,0:T(4,128)S(1)} %get-tuple-element.30), channel_id=1, source_target_pairs={{0,16},{16,32},{32,48},{48,64},{64,80},{80,96},{96,112},{112,128},... | collective-permute-start | bytes 73736 | tf_op jit(solution)/shard_map/ppermute | solution.py:19
  179.8 37.0 %all_gather.12 = f32[64,8,128]{2,1,0:T(8,128)} all-gather(f32[4,8,128]{2,1,0:T(8,128)S(1)} %get-tuple-element.14), channel_id=1, replica_groups=mesh['tile'=32,'dir'=16] {'dir'}, dimensions={0}, use_global_device_ids=true | all-gather | bytes 278528 | tf_op jit(solution)/shard_map/all_gather | solution.py:136
  218.3 3.6 collective-permute-start.15
  224.2 5.3 select_maximum_fusion.6
  232.5 7.7 %multiply_add_fusion.3 = f32[4,64,8,128]{3,2,1,0:T(8,128)S(1)} fusion(f32[4,64,8,128]{3,2,1,0:T(8,128)S(1)} %bitcast.132, f32[4,72,16,136]{3,2,1,0:T(8,128)S(1)} %copy-done.2, f32[4,64,4,128]{3,2,1,0:T(4,128)S(1)} %copy-done.15, f32[4,64,8,128]{3,2,1,0:T(8,128)S(1)} %convert_element_type.62, f32[4,64,4,128]{3,2,1,0:T(4,128)} %collective-permute-done, ...), kind=kLoop, calls=%fused_computation.110 | loop fusion | flops 23855104 | bytes 22806528 | tf_op jit(solution)/shard_map/add | solution.py:143
  246.3 7.5 collective-permute-start.16
  253.7 49.0 %all_gather.13 = f32[64,8,128]{2,1,0:T(8,128)S(1)} all-gather(f32[4,8,128]{2,1,0:T(8,128)S(1)} %get-tuple-element.12), channel_id=1, replica_groups=mesh['tile'=32,'dir'=16] {'dir'}, dimensions={0}, use_global_device_ids=true | all-gather | bytes 278528 | tf_op jit(solution)/shard_map/all_gather | solution.py:136
  305.5 6.1 multiply_add_fusion.2
  324.5 46.2 %all_gather.14 = f32[64,8,128]{2,1,0:T(8,128)S(1)} all-gather(f32[4,8,128]{2,1,0:T(8,128)S(1)} %get-tuple-element.10), channel_id=1, replica_groups=mesh['tile'=32,'dir'=16] {'dir'}, dimensions={0}, use_global_device_ids=true | all-gather | bytes 278528 | tf_op jit(solution)/shard_map/all_gather | solution.py:136
  372.0 3.2 collective-permute-start.22
  377.9 6.1 multiply_add_fusion.1
  387.4 11.4 %collective-permute-start.18 = (f32[4,64,4,128]{3,2,1,0:T(4,128)}, f32[4,64,4,128]{3,2,1,0:T(4,128)}, u32[]{:S(2)}, u32[]{:S(2)}) collective-permute-start(f32[4,64,4,128]{3,2,1,0:T(4,128)} %get-tuple-element.15), channel_id=1, source_target_pairs={{0,16},{16,32},{32,48},{48,64},{64,80},{80,96},{96,112},{112,128},... | collective-permute-start | bytes 1572872 | tf_op jit(solution)/shard_map/ppermute | solution.py:19
  399.7 48.9 %all_gather.15 = f32[64,8,128]{2,1,0:T(8,128)} all-gather(f32[4,8,128]{2,1,0:T(8,128)S(1)} %fusion.56), channel_id=1, replica_groups=mesh['tile'=32,'dir'=16] {'dir'}, dimensions={0}, use_global_device_ids=true | all-gather | bytes 278528 | tf_op jit(solution)/shard_map/all_gather | solution.py:136
  448.6 15.9 %copy.45 = f32[4,64,8,128]{0,3,2,1:T(8,128)} copy(f32[4,64,8,128]{3,2,1,0:T(8,128)S(1)} %multiply_add_fusion.3) | data formatting | bytes 2097152 | tf_op jit(solution)/shard_map/add | solution.py:143
  464.6 11.3 %gather_fusion = f32[256,4]{1,0:T(8,128)S(1)} fusion(f32[4,65536]{0,1:T(8,128)} %bitcast.128, s32[1024]{0:T(1024)S(1)} %pad_clamp_fusion), kind=kCustom, calls=%fused_computation.clone | custom fusion | bytes 9216 | tf_op jit(solution)/shard_map/jit(_take)/gather | solution.py:149
  475.8 16.0 %copy.46 = f32[4,64,8,128]{0,3,2,1:T(8,128)} copy(f32[4,64,8,128]{3,2,1,0:T(8,128)S(1)} %multiply_add_fusion.2) | data formatting | bytes 2097152 | tf_op jit(solution)/shard_map/add | solution.py:143
  491.8 11.9 %gather_fusion.1 = f32[256,4]{1,0:T(8,128)} fusion(f32[4,65536]{0,1:T(8,128)} %bitcast.130, s32[1024]{0:T(1024)S(1)} %pad_clamp_fusion), kind=kCustom, calls=%fused_computation.1.clone | custom fusion | bytes 9216 | tf_op jit(solution)/shard_map/jit(_take)/gather | solution.py:149
  503.7 16.0 %copy.47 = f32[4,64,8,128]{0,3,2,1:T(8,128)} copy(f32[4,64,8,128]{3,2,1,0:T(8,128)S(1)} %copy-done.4) | data formatting | bytes 2097152 | tf_op jit(solution)/shard_map/add | solution.py:143
  519.7 11.9 %gather_fusion.2 = f32[256,4]{1,0:T(8,128)} fusion(f32[4,65536]{0,1:T(8,128)} %bitcast.131, s32[1024]{0:T(1024)S(1)} %pad_clamp_fusion), kind=kCustom, calls=%fused_computation.2.clone | custom fusion | bytes 9216 | tf_op jit(solution)/shard_map/jit(_take)/gather | solution.py:149
  531.6 3.8 select_maximum_fusion
  535.4 8.5 %multiply_add_fusion = f32[4,64,8,128]{3,2,1,0:T(8,128)} fusion(f32[4,64,8,128]{3,2,1,0:T(8,128)S(1)} %bitcast.135, f32[4,72,16,136]{3,2,1,0:T(8,128)S(1)} %select_maximum_fusion, f32[4,64,4,128]{3,2,1,0:T(4,128)} %collective-permute-done.19, f32[4,64,8,128]{3,2,1,0:T(8,128)S(1)} %copy-done.4, f32[4,64,4,128]{3,2,1,0:T(4,128)} %collective-permute-done.18, ...), kind=kLoop, calls=%fused_computation.107 | loop fusion | flops 23592960 | bytes 23330816 | tf_op jit(solution)/shard_map/add | solution.py:143
  543.9 16.9 %copy.48 = f32[4,64,8,128]{0,3,2,1:T(8,128)} copy(f32[4,64,8,128]{3,2,1,0:T(8,128)} %multiply_add_fusion) | data formatting | bytes 2097152 | tf_op jit(solution)/shard_map/add | solution.py:143
  560.8 11.3 %gather_fusion.3 = f32[256,4]{1,0:T(8,128)S(1)} fusion(f32[4,65536]{0,1:T(8,128)} %bitcast.129, s32[1024]{0:T(1024)S(1)} %pad_clamp_fusion), kind=kCustom, calls=%fused_computation.3.clone | custom fusion | bytes 9216 | tf_op jit(solution)/shard_map/jit(_take)/gather | solution.py:149
  572.6 173.6 %psum.7 = f32[4,4,256]{2,1,0:T(4,128)} all-reduce(f32[4,4,256]{2,1,0:T(4,128)S(1)} %pad_maximum_fusion.12), channel_id=1, replica_groups=mesh['tile'=32,'dir'=16] {'tile'}, use_global_device_ids=true, to_apply=%region_1.3 | all-reduce | flops 4096 | bytes 32768 | tf_op jit(solution)/shard_map/psum | solution.py:153
  (143 shorter events, 62.8 us)
Async XLA Ops:
  3.8 32.4 %all-to-all-start = ((bf16[1,32,2]{2,0,1:T(2,128)(2,1)}), bf16[1,32,2]{2,0,1:T(2,128)(2,1)S(1)}, u32[]{:S(2)}, u32[]{:S(2)}) async-start(bf16[1,32,2]{2,0,1:T(2,128)(2,1)} %all_to_all.12), calls=%async_computation | async-start | bytes 32768 | tf_op jit(solution)/shard_map/all_to_all | solution.py:74
  25.4 105.0 %copy-start.20 = (bf16[64,8,128]{2,1,0:T(8,128)(2,1)S(1)}, bf16[64,8,128]{2,1,0:T(8,128)(2,1)}, u32[]{:S(2)}) copy-start(bf16[64,8,128]{2,1,0:T(8,128)(2,1)} %param.18) | copy-start | bytes 393220
  36.3 193.2 %all-to-all-start.1 = ((bf16[4,64,32,128]{3,2,0,1:T(8,128)(2,1)}), bf16[4,64,32,128]{3,2,0,1:T(8,128)(2,1)}, u32[]{:S(2)}, u32[]{:S(2)}) async-start(bf16[4,64,32,128]{3,2,0,1:T(8,128)(2,1)} %copy.42), calls=%async_computation.1 | async-start | bytes 4194304 | tf_op jit(solution)/shard_map/all_to_all | solution.py:73
  41.8 83.6 %collective-permute-start.3 = (f32[1,4,8,128]{3,2,1,0:T(8,128)S(1)}, f32[1,4,8,128]{3,2,1,0:T(8,128)S(1)}, u32[]{:S(2)}, u32[]{:S(2)}) collective-permute-start(f32[1,4,8,128]{3,2,1,0:T(8,128)S(1)} %dynamic-slice_bitcast_fusion.3), channel_id=1, source_target_pairs={{1,0},{2,1},{3,2},{4,3},{5,4},{6,5},{7,6},{8,7},{9,8},{10,9},{11,1... | collective-permute-start | bytes 49160 | tf_op jit(solution)/shard_map/ppermute | solution.py:22
  45.8 79.6 %collective-permute-start.2 = (f32[1,4,8,128]{3,2,1,0:T(8,128)S(1)}, f32[1,4,8,128]{3,2,1,0:T(8,128)S(1)}, u32[]{:S(2)}, u32[]{:S(2)}) collective-permute-start(f32[1,4,8,128]{3,2,1,0:T(8,128)S(1)} %dynamic-slice_bitcast_fusion.3), channel_id=1, source_target_pairs={{0,1},{1,2},{2,3},{3,4},{4,5},{5,6},{6,7},{7,8},{8,9},{9,10},{10,1... | collective-permute-start | bytes 49160 | tf_op jit(solution)/shard_map/ppermute | solution.py:19
  48.8 175.3 %collective-permute-start.1 = (f32[4,64,4,128]{3,2,1,0:T(4,128)}, f32[4,64,4,128]{3,2,1,0:T(4,128)S(1)}, u32[]{:S(2)}, u32[]{:S(2)}) collective-permute-start(f32[4,64,4,128]{3,2,1,0:T(4,128)} %get-tuple-element.25), channel_id=1, source_target_pairs={{16,0},{32,16},{48,32},{64,48},{80,64},{96,80},{112,96},{128,112},... | collective-permute-start | bytes 1572872 | tf_op jit(solution)/shard_map/ppermute | solution.py:22
  50.1 174.0 %collective-permute-start = (f32[4,64,4,128]{3,2,1,0:T(4,128)}, f32[4,64,4,128]{3,2,1,0:T(4,128)}, u32[]{:S(2)}, u32[]{:S(2)}) collective-permute-start(f32[4,64,4,128]{3,2,1,0:T(4,128)} %get-tuple-element.24), channel_id=1, source_target_pairs={{0,16},{16,32},{32,48},{48,64},{64,80},{80,96},{96,112},{112,128},... | collective-permute-start | bytes 1572872 | tf_op jit(solution)/shard_map/ppermute | solution.py:19
  54.0 175.4 %copy-start.13 = (f32[3,64,8,128]{3,2,1,0:T(8,128)}, f32[3,64,8,128]{3,2,1,0:T(8,128)S(1)}, u32[]{:S(2)}) copy-start(f32[3,64,8,128]{3,2,1,0:T(8,128)S(1)} %convert_element_type.65) | copy-start | bytes 2359300
  125.4 5.1 collective-permute-start.5
  126.7 3.9 collective-permute-start.4
  132.1 29.7 %collective-permute-start.9 = (f32[1,4,8,128]{3,2,1,0:T(8,128)S(1)}, f32[1,4,8,128]{3,2,1,0:T(8,128)S(1)}, u32[]{:S(2)}, u32[]{:S(2)}) collective-permute-start(f32[1,4,8,128]{3,2,1,0:T(8,128)S(1)} %bitcast.136), channel_id=1, source_target_pairs={{1,0},{2,1},{3,2},{4,3},{5,4},{6,5},{7,6},{8,7},{9,8},{10,9},{11,1... | collective-permute-start | bytes 49160 | tf_op jit(solution)/shard_map/ppermute | solution.py:22
  159.8 8.3 %collective-permute-start.8 = (f32[1,4,8,128]{3,2,1,0:T(8,128)S(1)}, f32[1,4,8,128]{3,2,1,0:T(8,128)S(1)}, u32[]{:S(2)}, u32[]{:S(2)}) collective-permute-start(f32[1,4,8,128]{3,2,1,0:T(8,128)S(1)} %bitcast.137), channel_id=1, source_target_pairs={{0,1},{1,2},{2,3},{3,4},{4,5},{5,6},{6,7},{7,8},{8,9},{9,10},{10,1... | collective-permute-start | bytes 49160 | tf_op jit(solution)/shard_map/ppermute | solution.py:19
  168.1 48.6 %collective-permute-start.11 = (f32[1,12,4,128]{3,2,1,0:T(4,128)S(1)}, f32[1,12,4,128]{3,2,1,0:T(4,128)S(1)}, u32[]{:S(2)}, u32[]{:S(2)}) collective-permute-start(f32[1,12,4,128]{3,2,1,0:T(4,128)S(1)} %get-tuple-element.31), channel_id=1, source_target_pairs={{16,0},{32,16},{48,32},{64,48},{80,64},{96,80},{112,96},{128,112},... | collective-permute-start | bytes 73736 | tf_op jit(solution)/shard_map/ppermute | solution.py:22
  169.4 47.3 %collective-permute-start.10 = (f32[1,12,4,128]{3,2,1,0:T(4,128)S(1)}, f32[1,12,4,128]{3,2,1,0:T(4,128)S(1)}, u32[]{:S(2)}, u32[]{:S(2)}) collective-permute-start(f32[1,12,4,128]{3,2,1,0:T(4,128)S(1)} %get-tuple-element.30), channel_id=1, source_target_pairs={{0,16},{16,32},{32,48},{48,64},{64,80},{80,96},{96,112},{112,128},... | collective-permute-start | bytes 73736 | tf_op jit(solution)/shard_map/ppermute | solution.py:19
  218.3 26.6 %collective-permute-start.15 = (f32[1,4,8,128]{3,2,1,0:T(8,128)S(1)}, f32[1,4,8,128]{3,2,1,0:T(8,128)S(1)}, u32[]{:S(2)}, u32[]{:S(2)}) collective-permute-start(f32[1,4,8,128]{3,2,1,0:T(8,128)S(1)} %get-tuple-element.11), channel_id=1, source_target_pairs={{1,0},{2,1},{3,2},{4,3},{5,4},{6,5},{7,6},{8,7},{9,8},{10,9},{11,1... | collective-permute-start | bytes 49160 | tf_op jit(solution)/shard_map/ppermute | solution.py:22
  221.9 23.0 %collective-permute-start.14 = (f32[1,4,8,128]{3,2,1,0:T(8,128)S(1)}, f32[1,4,8,128]{3,2,1,0:T(8,128)S(1)}, u32[]{:S(2)}, u32[]{:S(2)}) collective-permute-start(f32[1,4,8,128]{3,2,1,0:T(8,128)S(1)} %get-tuple-element.11), channel_id=1, source_target_pairs={{0,1},{1,2},{2,3},{3,4},{4,5},{5,6},{6,7},{7,8},{8,9},{9,10},{10,1... | collective-permute-start | bytes 49160 | tf_op jit(solution)/shard_map/ppermute | solution.py:19
  240.2 65.2 %copy-start.6 = (bf16[4,64,8,128]{3,2,1,0:T(8,128)(2,1)S(1)}, bf16[4,64,8,128]{3,2,1,0:T(8,128)(2,1)}, u32[]{:S(2)}) copy-start(bf16[4,64,8,128]{3,2,1,0:T(8,128)(2,1)} %param.21) | copy-start | bytes 1572868
  240.2 65.2 %copy-start.7 = (f32[64,8,128]{2,1,0:T(8,128)S(1)}, f32[64,8,128]{2,1,0:T(8,128)}, u32[]{:S(2)}) copy-start(f32[64,8,128]{2,1,0:T(8,128)} %get-tuple-element.21) | copy-start | bytes 786436
  240.2 65.2 %copy-start.9 = (f32[64,8,128]{2,1,0:T(8,128)S(1)}, f32[64,8,128]{2,1,0:T(8,128)}, u32[]{:S(2)}) copy-start(f32[64,8,128]{2,1,0:T(8,128)} %get-tuple-element.22) | copy-start | bytes 786436
  240.4 62.3 %collective-permute-start.7 = (f32[4,64,4,128]{3,2,1,0:T(4,128)S(1)}, f32[4,64,4,128]{3,2,1,0:T(4,128)S(1)}, u32[]{:S(2)}, u32[]{:S(2)}) collective-permute-start(f32[4,64,4,128]{3,2,1,0:T(4,128)S(1)} %get-tuple-element.20), channel_id=1, source_target_pairs={{16,0},{32,16},{48,32},{64,48},{80,64},{96,80},{112,96},{128,112},... | collective-permute-start | bytes 1572872 | tf_op jit(solution)/shard_map/ppermute | solution.py:22
  241.9 60.9 %collective-permute-start.6 = (f32[4,64,4,128]{3,2,1,0:T(4,128)S(1)}, f32[4,64,4,128]{3,2,1,0:T(4,128)S(1)}, u32[]{:S(2)}, u32[]{:S(2)}) collective-permute-start(f32[4,64,4,128]{3,2,1,0:T(4,128)S(1)} %get-tuple-element.19), channel_id=1, source_target_pairs={{0,16},{16,32},{32,48},{48,64},{64,80},{80,96},{96,112},{112,128},... | collective-permute-start | bytes 1572872 | tf_op jit(solution)/shard_map/ppermute | solution.py:19
  245.0 57.7 %collective-permute-start.17 = (f32[1,12,4,128]{3,2,1,0:T(4,128)S(1)}, f32[1,12,4,128]{3,2,1,0:T(4,128)S(1)}, u32[]{:S(2)}, u32[]{:S(2)}) collective-permute-start(f32[1,12,4,128]{3,2,1,0:T(4,128)S(1)} %get-tuple-element.29), channel_id=1, source_target_pairs={{16,0},{32,16},{48,32},{64,48},{80,64},{96,80},{112,96},{128,112},... | collective-permute-start | bytes 73736 | tf_op jit(solution)/shard_map/ppermute | solution.py:22
  246.3 56.4 %collective-permute-start.16 = (f32[1,12,4,128]{3,2,1,0:T(4,128)S(1)}, f32[1,12,4,128]{3,2,1,0:T(4,128)S(1)}, u32[]{:S(2)}, u32[]{:S(2)}) collective-permute-start(f32[1,12,4,128]{3,2,1,0:T(4,128)S(1)} %get-tuple-element.28), channel_id=1, source_target_pairs={{0,16},{16,32},{32,48},{48,64},{64,80},{80,96},{96,112},{112,128},... | collective-permute-start | bytes 73736 | tf_op jit(solution)/shard_map/ppermute | solution.py:19
  311.8 63.4 %collective-permute-start.13 = (f32[4,64,4,128]{3,2,1,0:T(4,128)S(1)}, f32[4,64,4,128]{3,2,1,0:T(4,128)S(1)}, u32[]{:S(2)}, u32[]{:S(2)}) collective-permute-start(f32[4,64,4,128]{3,2,1,0:T(4,128)S(1)} %get-tuple-element.18), channel_id=1, source_target_pairs={{16,0},{32,16},{48,32},{64,48},{80,64},{96,80},{112,96},{128,112},... | collective-permute-start | bytes 1572872 | tf_op jit(solution)/shard_map/ppermute | solution.py:22
  313.1 62.1 %collective-permute-start.12 = (f32[4,64,4,128]{3,2,1,0:T(4,128)S(1)}, f32[4,64,4,128]{3,2,1,0:T(4,128)S(1)}, u32[]{:S(2)}, u32[]{:S(2)}) collective-permute-start(f32[4,64,4,128]{3,2,1,0:T(4,128)S(1)} %get-tuple-element.17), channel_id=1, source_target_pairs={{0,16},{16,32},{32,48},{48,64},{64,80},{80,96},{96,112},{112,128},... | collective-permute-start | bytes 1572872 | tf_op jit(solution)/shard_map/ppermute | solution.py:19
  318.4 52.3 %collective-permute-start.21 = (f32[1,4,8,128]{3,2,1,0:T(8,128)S(1)}, f32[1,4,8,128]{3,2,1,0:T(8,128)S(1)}, u32[]{:S(2)}, u32[]{:S(2)}) collective-permute-start(f32[1,4,8,128]{3,2,1,0:T(8,128)S(1)} %get-tuple-element.9), channel_id=1, source_target_pairs={{1,0},{2,1},{3,2},{4,3},{5,4},{6,5},{7,6},{8,7},{9,8},{10,9},{11,1... | collective-permute-start | bytes 49160 | tf_op jit(solution)/shard_map/ppermute | solution.py:22
  321.5 49.1 %collective-permute-start.20 = (f32[1,4,8,128]{3,2,1,0:T(8,128)S(1)}, f32[1,4,8,128]{3,2,1,0:T(8,128)S(1)}, u32[]{:S(2)}, u32[]{:S(2)}) collective-permute-start(f32[1,4,8,128]{3,2,1,0:T(8,128)S(1)} %get-tuple-element.9), channel_id=1, source_target_pairs={{0,1},{1,2},{2,3},{3,4},{4,5},{5,6},{6,7},{7,8},{8,9},{9,10},{10,1... | collective-permute-start | bytes 49160 | tf_op jit(solution)/shard_map/ppermute | solution.py:19
  370.7 28.1 %collective-permute-start.23 = (f32[1,12,4,128]{3,2,1,0:T(4,128)S(1)}, f32[1,12,4,128]{3,2,1,0:T(4,128)S(1)}, u32[]{:S(2)}, u32[]{:S(2)}) collective-permute-start(f32[1,12,4,128]{3,2,1,0:T(4,128)S(1)} %get-tuple-element.27), channel_id=1, source_target_pairs={{16,0},{32,16},{48,32},{64,48},{80,64},{96,80},{112,96},{128,112},... | collective-permute-start | bytes 73736 | tf_op jit(solution)/shard_map/ppermute | solution.py:22
  372.0 26.8 %collective-permute-start.22 = (f32[1,12,4,128]{3,2,1,0:T(4,128)S(1)}, f32[1,12,4,128]{3,2,1,0:T(4,128)S(1)}, u32[]{:S(2)}, u32[]{:S(2)}) collective-permute-start(f32[1,12,4,128]{3,2,1,0:T(4,128)S(1)} %get-tuple-element.26), channel_id=1, source_target_pairs={{0,16},{16,32},{32,48},{48,64},{64,80},{80,96},{96,112},{112,128},... | collective-permute-start | bytes 73736 | tf_op jit(solution)/shard_map/ppermute | solution.py:19
  386.1 145.5 %collective-permute-start.19 = (f32[4,64,4,128]{3,2,1,0:T(4,128)}, f32[4,64,4,128]{3,2,1,0:T(4,128)}, u32[]{:S(2)}, u32[]{:S(2)}) collective-permute-start(f32[4,64,4,128]{3,2,1,0:T(4,128)} %get-tuple-element.16), channel_id=1, source_target_pairs={{16,0},{32,16},{48,32},{64,48},{80,64},{96,80},{112,96},{128,112},... | collective-permute-start | bytes 1572872 | tf_op jit(solution)/shard_map/ppermute | solution.py:22
  387.4 144.2 %collective-permute-start.18 = (f32[4,64,4,128]{3,2,1,0:T(4,128)}, f32[4,64,4,128]{3,2,1,0:T(4,128)}, u32[]{:S(2)}, u32[]{:S(2)}) collective-permute-start(f32[4,64,4,128]{3,2,1,0:T(4,128)} %get-tuple-element.15), channel_id=1, source_target_pairs={{0,16},{16,32},{32,48},{48,64},{64,80},{80,96},{96,112},{112,128},... | collective-permute-start | bytes 1572872 | tf_op jit(solution)/shard_map/ppermute | solution.py:19
  543.9 202.3 %copy-start.1 = (bf16[4,32,32,128]{3,2,1,0:T(8,128)(2,1)S(1)}, bf16[4,32,32,128]{3,2,1,0:T(8,128)(2,1)}, u32[]{:S(2)}) copy-start(bf16[4,32,32,128]{3,2,1,0:T(8,128)(2,1)} %param.22) | copy-start | bytes 3145732
  (20 other events, 408.1 us)
where the time goes:
time: 748 us; the launch traced here: 746 us
  blocking collectives  355 us (47%)
  starting transfers between devices  126 us (17%)
  local copies, waits for them, and re-layouts  122 us (16%)
  waiting for transfers between devices  84.8 us (11%)
  other arithmetic  52.8 us (7%)
    all_gather x4, blocking collectives, local(): acceleration = lax.all_gather(local_accel, 'dir', axis=0, tiled=True)  181 us
    psum x1, blocking collectives, local(): traces = lax.psum(jnp.stack(records, axis=1), 'tile')  174 us
    ppermute x12, waiting for transfers between devices, padded_2(): lax.ppermute(lax.slice_in_dim(block, 0, width, axis=dim), axis, backward)  67.6 us
    add x4, local copies, waits for them, and re-layouts, local(): 2.0 * current_born - earlier_born  64.7 us
    ppermute x12, starting transfers between devices, padded_2(): lax.ppermute(lax.slice_in_dim(block, block.shape[dim] - width, None, axis...  54.4 us
    ppermute x12, starting transfers between devices, padded_2(): lax.ppermute(lax.slice_in_dim(block, 0, width, axis=dim), axis, backward)  48.9 us
    gather x4, local copies, waits for them, and re-layouts, local(): jnp.take(following.reshape(following.shape[0], -1), flat_index, axis=1)  46.3 us
    add x4, other arithmetic, local(): 2.0 * current_born - earlier_born  28.4 us
  transfers between devices with their start and end apart: 26, of which 4 were waited for; matrix products, arithmetic and copies ran while one was open for 17% of the time, Pallas kernels for 0%

commit v1 on v0

--- a/solution.py
+++ b/solution.py
@@ -150,7 +150,8 @@
             * inside[None, :]
         )
         earlier_born, current_born = (current_born, following)
-    traces = lax.psum(jnp.stack(records, axis=1), "tile")
+    make_field_on_mesh = lambda slab_in: jnp.sum(lax.all_gather(slab_in, "tile"), axis=0)
+    traces = make_field_on_mesh(jnp.stack(records, axis=1))
     return (current_born, traces)
 
 

time: 748 us -> 638 us (0.85)
  blocking collectives: 355 us -> 238 us
    psum x1 -> x0, blocking collectives: 174 us -> none  [local(): traces = lax.psum(jnp.stack(records, axis=1), 'tile')]
    all_gather x0 -> x1, blocking collectives: none -> 57.3 us  [local(): lax.all_gather(slab_in, 'tile')]
  transfers between devices with their start and end apart: 26 -> 26, of which waited for: 4 -> 4; matrix products, arithmetic and copies ran while one was open for 17% -> 20% of each run, Pallas kernels for 0% -> 0%
where the time goes in v1:
time: 638 us; the launch traced here: 631 us
  blocking collectives  238 us (37%)
  starting transfers between devices  126 us (20%)
  local copies, waits for them, and re-layouts  122 us (19%)
  waiting for transfers between devices  84.8 us (13%)
  other arithmetic  53.5 us (8%)
    all_gather x4, blocking collectives, local(): acceleration = lax.all_gather(local_accel, 'dir', axis=0, tiled=True)  181 us
    ppermute x12, waiting for transfers between devices, padded_2(): lax.ppermute(lax.slice_in_dim(block, 0, width, axis=dim), axis, backward)  67.6 us
    add x4, local copies, waits for them, and re-layouts, local(): 2.0 * current_born - earlier_born  64.7 us
    all_gather x1, blocking collectives, local(): lax.all_gather(slab_in, 'tile')  57.3 us
    ppermute x12, starting transfers between devices, padded_2(): lax.ppermute(lax.slice_in_dim(block, block.shape[dim] - width, None, axis...  54.4 us
    ppermute x12, starting transfers between devices, padded_2(): lax.ppermute(lax.slice_in_dim(block, 0, width, axis=dim), axis, backward)  48.9 us
    gather x4, local copies, waits for them, and re-layouts, local(): jnp.take(following.reshape(following.shape[0], -1), flat_index, axis=1)  46.3 us
    add x4, other arithmetic, local(): 2.0 * current_born - earlier_born  28.4 us
  transfers between devices with their start and end apart: 26, of which 4 were waited for; matrix products, arithmetic and copies ran while one was open for 20% of the time, Pallas kernels for 0%

profile of v1, /device:TPU:24, one launch (start us, length us, event | category | flops | bytes accessed | tf_op | source)
XLA Modules:
  0.0 630.6 jit_solution(17042218702430523955)
XLA Ops:
  3.8 17.9 %all-to-all-start = ((bf16[1,32,2]{2,0,1:T(2,128)(2,1)}), bf16[1,32,2]{2,0,1:T(2,128)(2,1)S(1)}, u32[]{:S(2)}, u32[]{:S(2)}) async-start(bf16[1,32,2]{2,0,1:T(2,128)(2,1)} %all_to_all.12), calls=%async_computation | async-start | bytes 32768 | tf_op jit(solution)/shard_map/all_to_all | solution.py:74
  25.4 10.8 %all-to-all-done = bf16[1,32,2]{2,0,1:T(2,128)(2,1)S(1)} async-done(((bf16[1,32,2]{2,0,1:T(2,128)(2,1)}), bf16[1,32,2]{2,0,1:T(2,128)(2,1)S(1)}, u32[]{:S(2)}, u32[]{:S(2)}) %all-to-all-start) | async-done | bytes 160 | tf_op jit(solution)/shard_map/all_to_all | solution.py:74
  36.3 4.8 all-to-all-start.1
  41.8 4.0 collective-permute-start.3
  50.1 3.8 collective-permute-start
  57.7 67.6 %collective-permute-done.3 = f32[1,4,8,128]{3,2,1,0:T(8,128)S(1)} collective-permute-done((f32[1,4,8,128]{3,2,1,0:T(8,128)S(1)}, f32[1,4,8,128]{3,2,1,0:T(8,128)S(1)}, u32[]{:S(2)}, u32[]{:S(2)}) %collective-permute-start.3) | collective-permute-done | bytes 16416 | tf_op jit(solution)/shard_map/ppermute | solution.py:22
  132.1 27.6 %collective-permute-start.9 = (f32[1,4,8,128]{3,2,1,0:T(8,128)S(1)}, f32[1,4,8,128]{3,2,1,0:T(8,128)S(1)}, u32[]{:S(2)}, u32[]{:S(2)}) collective-permute-start(f32[1,4,8,128]{3,2,1,0:T(8,128)S(1)} %bitcast.138), channel_id=1, source_target_pairs={{1,0},{2,1},{3,2},{4,3},{5,4},{6,5},{7,6},{8,7},{9,8},{10,9},{11,1... | collective-permute-start | bytes 49160 | tf_op jit(solution)/shard_map/ppermute | solution.py:22
  161.9 6.2 collective-permute-done.8
  169.4 10.4 %collective-permute-start.10 = (f32[1,12,4,128]{3,2,1,0:T(4,128)S(1)}, f32[1,12,4,128]{3,2,1,0:T(4,128)S(1)}, u32[]{:S(2)}, u32[]{:S(2)}) collective-permute-start(f32[1,12,4,128]{3,2,1,0:T(4,128)S(1)} %get-tuple-element.26), channel_id=1, source_target_pairs={{0,16},{16,32},{32,48},{48,64},{64,80},{80,96},{96,112},{112,128},... | collective-permute-start | bytes 73736 | tf_op jit(solution)/shard_map/ppermute | solution.py:19
  179.8 37.0 %all_gather.18 = f32[64,8,128]{2,1,0:T(8,128)} all-gather(f32[4,8,128]{2,1,0:T(8,128)S(1)} %get-tuple-element.10), channel_id=1, replica_groups=mesh['tile'=32,'dir'=16] {'dir'}, dimensions={0}, use_global_device_ids=true | all-gather | bytes 278528 | tf_op jit(solution)/shard_map/all_gather | solution.py:136
  218.3 3.6 collective-permute-start.15
  224.2 5.3 select_maximum_fusion.6
  232.5 7.7 %multiply_add_fusion.3 = f32[4,64,8,128]{3,2,1,0:T(8,128)S(1)} fusion(f32[4,64,8,128]{3,2,1,0:T(8,128)S(1)} %bitcast.133, f32[4,72,16,136]{3,2,1,0:T(8,128)S(1)} %copy-done.2, f32[4,64,4,128]{3,2,1,0:T(4,128)S(1)} %copy-done.15, f32[4,64,8,128]{3,2,1,0:T(8,128)S(1)} %convert_element_type.62, f32[4,64,4,128]{3,2,1,0:T(4,128)} %collective-permute-done, ...), kind=kLoop, calls=%fused_computation.110 | loop fusion | flops 23855104 | bytes 22806528 | tf_op jit(solution)/shard_map/add | solution.py:143
  246.3 7.5 %collective-permute-start.16 = (f32[1,12,4,128]{3,2,1,0:T(4,128)S(1)}, f32[1,12,4,128]{3,2,1,0:T(4,128)S(1)}, u32[]{:S(2)}, u32[]{:S(2)}) collective-permute-start(f32[1,12,4,128]{3,2,1,0:T(4,128)S(1)} %get-tuple-element.24), channel_id=1, source_target_pairs={{0,16},{16,32},{32,48},{48,64},{64,80},{80,96},{96,112},{112,128},... | collective-permute-start | bytes 73736 | tf_op jit(solution)/shard_map/ppermute | solution.py:19
  253.7 49.0 %all_gather.19 = f32[64,8,128]{2,1,0:T(8,128)S(1)} all-gather(f32[4,8,128]{2,1,0:T(8,128)S(1)} %get-tuple-element.8), channel_id=1, replica_groups=mesh['tile'=32,'dir'=16] {'dir'}, dimensions={0}, use_global_device_ids=true | all-gather | bytes 278528 | tf_op jit(solution)/shard_map/all_gather | solution.py:136
  305.5 6.1 multiply_add_fusion.2
  324.5 46.2 %all_gather.20 = f32[64,8,128]{2,1,0:T(8,128)S(1)} all-gather(f32[4,8,128]{2,1,0:T(8,128)S(1)} %get-tuple-element.6), channel_id=1, replica_groups=mesh['tile'=32,'dir'=16] {'dir'}, dimensions={0}, use_global_device_ids=true | all-gather | bytes 278528 | tf_op jit(solution)/shard_map/all_gather | solution.py:136
  372.0 3.2 collective-permute-start.22
  377.9 6.1 multiply_add_fusion.1
  387.4 11.4 %collective-permute-start.18 = (f32[4,64,4,128]{3,2,1,0:T(4,128)}, f32[4,64,4,128]{3,2,1,0:T(4,128)}, u32[]{:S(2)}, u32[]{:S(2)}) collective-permute-start(f32[4,64,4,128]{3,2,1,0:T(4,128)} %get-tuple-element.11), channel_id=1, source_target_pairs={{0,16},{16,32},{32,48},{48,64},{64,80},{80,96},{96,112},{112,128},... | collective-permute-start | bytes 1572872 | tf_op jit(solution)/shard_map/ppermute | solution.py:19
  399.7 48.9 %all_gather.21 = f32[64,8,128]{2,1,0:T(8,128)} all-gather(f32[4,8,128]{2,1,0:T(8,128)S(1)} %fusion.56), channel_id=1, replica_groups=mesh['tile'=32,'dir'=16] {'dir'}, dimensions={0}, use_global_device_ids=true | all-gather | bytes 278528 | tf_op jit(solution)/shard_map/all_gather | solution.py:136
  448.6 15.9 %copy.44 = f32[4,64,8,128]{0,3,2,1:T(8,128)} copy(f32[4,64,8,128]{3,2,1,0:T(8,128)S(1)} %multiply_add_fusion.3) | data formatting | bytes 2097152 | tf_op jit(solution)/shard_map/add | solution.py:143
  464.6 11.3 %gather_fusion = f32[256,4]{1,0:T(8,128)S(1)} fusion(f32[4,65536]{0,1:T(8,128)} %bitcast.129, s32[1024]{0:T(1024)S(1)} %pad_clamp_fusion), kind=kCustom, calls=%fused_computation.clone | custom fusion | bytes 9216 | tf_op jit(solution)/shard_map/jit(_take)/gather | solution.py:149
  475.8 16.0 %copy.45 = f32[4,64,8,128]{0,3,2,1:T(8,128)} copy(f32[4,64,8,128]{3,2,1,0:T(8,128)S(1)} %multiply_add_fusion.2) | data formatting | bytes 2097152 | tf_op jit(solution)/shard_map/add | solution.py:143
  491.8 11.9 %gather_fusion.1 = f32[256,4]{1,0:T(8,128)} fusion(f32[4,65536]{0,1:T(8,128)} %bitcast.131, s32[1024]{0:T(1024)S(1)} %pad_clamp_fusion), kind=kCustom, calls=%fused_computation.1.clone | custom fusion | bytes 9216 | tf_op jit(solution)/shard_map/jit(_take)/gather | solution.py:149
  503.7 16.0 %copy.46 = f32[4,64,8,128]{0,3,2,1:T(8,128)} copy(f32[4,64,8,128]{3,2,1,0:T(8,128)S(1)} %copy-done.4) | data formatting | bytes 2097152 | tf_op jit(solution)/shard_map/add | solution.py:143
  519.7 11.9 %gather_fusion.2 = f32[256,4]{1,0:T(8,128)} fusion(f32[4,65536]{0,1:T(8,128)} %bitcast.132, s32[1024]{0:T(1024)S(1)} %pad_clamp_fusion), kind=kCustom, calls=%fused_computation.2.clone | custom fusion | bytes 9216 | tf_op jit(solution)/shard_map/jit(_take)/gather | solution.py:149
  531.6 3.8 select_maximum_fusion
  535.4 8.5 %multiply_add_fusion = f32[4,64,8,128]{3,2,1,0:T(8,128)} fusion(f32[4,64,8,128]{3,2,1,0:T(8,128)S(1)} %bitcast.136, f32[4,72,16,136]{3,2,1,0:T(8,128)S(1)} %select_maximum_fusion, f32[4,64,4,128]{3,2,1,0:T(4,128)} %collective-permute-done.19, f32[4,64,8,128]{3,2,1,0:T(8,128)S(1)} %copy-done.4, f32[4,64,4,128]{3,2,1,0:T(4,128)} %collective-permute-done.18, ...), kind=kLoop, calls=%fused_computation.107 | loop fusion | flops 23592960 | bytes 23330816 | tf_op jit(solution)/shard_map/add | solution.py:143
  543.9 16.9 %copy.47 = f32[4,64,8,128]{0,3,2,1:T(8,128)} copy(f32[4,64,8,128]{3,2,1,0:T(8,128)} %multiply_add_fusion) | data formatting | bytes 2097152 | tf_op jit(solution)/shard_map/add | solution.py:143
  560.8 11.3 %gather_fusion.3 = f32[256,4]{1,0:T(8,128)S(1)} fusion(f32[4,65536]{0,1:T(8,128)} %bitcast.130, s32[1024]{0:T(1024)S(1)} %pad_clamp_fusion), kind=kCustom, calls=%fused_computation.3.clone | custom fusion | bytes 9216 | tf_op jit(solution)/shard_map/jit(_take)/gather | solution.py:149
  572.6 57.3 %all-gather = f32[128,4,256]{2,1,0:T(4,128)S(1)} all-gather(f32[4,4,256]{2,1,0:T(4,128)S(1)} %pad_maximum_fusion.12), channel_id=2, replica_groups=mesh['tile'=32,'dir'=16] {'tile'}, dimensions={0}, use_global_device_ids=true | all-gather | bytes 540672 | tf_op jit(solution)/shard_map/all_gather | solution.py:153
  (144 shorter events, 63.5 us)
Async XLA Ops:
  3.8 32.4 %all-to-all-start = ((bf16[1,32,2]{2,0,1:T(2,128)(2,1)}), bf16[1,32,2]{2,0,1:T(2,128)(2,1)S(1)}, u32[]{:S(2)}, u32[]{:S(2)}) async-start(bf16[1,32,2]{2,0,1:T(2,128)(2,1)} %all_to_all.12), calls=%async_computation | async-start | bytes 32768 | tf_op jit(solution)/shard_map/all_to_all | solution.py:74
  25.4 105.0 %copy-start.20 = (bf16[64,8,128]{2,1,0:T(8,128)(2,1)S(1)}, bf16[64,8,128]{2,1,0:T(8,128)(2,1)}, u32[]{:S(2)}) copy-start(bf16[64,8,128]{2,1,0:T(8,128)(2,1)} %param.18) | copy-start | bytes 393220
  36.3 193.2 %all-to-all-start.1 = ((bf16[4,64,32,128]{3,2,0,1:T(8,128)(2,1)}), bf16[4,64,32,128]{3,2,0,1:T(8,128)(2,1)}, u32[]{:S(2)}, u32[]{:S(2)}) async-start(bf16[4,64,32,128]{3,2,0,1:T(8,128)(2,1)} %copy.41), calls=%async_computation.1 | async-start | bytes 4194304 | tf_op jit(solution)/shard_map/all_to_all | solution.py:73
  41.8 83.6 %collective-permute-start.3 = (f32[1,4,8,128]{3,2,1,0:T(8,128)S(1)}, f32[1,4,8,128]{3,2,1,0:T(8,128)S(1)}, u32[]{:S(2)}, u32[]{:S(2)}) collective-permute-start(f32[1,4,8,128]{3,2,1,0:T(8,128)S(1)} %dynamic-slice_bitcast_fusion.3), channel_id=1, source_target_pairs={{1,0},{2,1},{3,2},{4,3},{5,4},{6,5},{7,6},{8,7},{9,8},{10,9},{11,1... | collective-permute-start | bytes 49160 | tf_op jit(solution)/shard_map/ppermute | solution.py:22
  45.8 79.6 %collective-permute-start.2 = (f32[1,4,8,128]{3,2,1,0:T(8,128)S(1)}, f32[1,4,8,128]{3,2,1,0:T(8,128)S(1)}, u32[]{:S(2)}, u32[]{:S(2)}) collective-permute-start(f32[1,4,8,128]{3,2,1,0:T(8,128)S(1)} %dynamic-slice_bitcast_fusion.3), channel_id=1, source_target_pairs={{0,1},{1,2},{2,3},{3,4},{4,5},{5,6},{6,7},{7,8},{8,9},{9,10},{10,1... | collective-permute-start | bytes 49160 | tf_op jit(solution)/shard_map/ppermute | solution.py:19
  48.8 175.3 %collective-permute-start.1 = (f32[4,64,4,128]{3,2,1,0:T(4,128)}, f32[4,64,4,128]{3,2,1,0:T(4,128)S(1)}, u32[]{:S(2)}, u32[]{:S(2)}) collective-permute-start(f32[4,64,4,128]{3,2,1,0:T(4,128)} %get-tuple-element.21), channel_id=1, source_target_pairs={{16,0},{32,16},{48,32},{64,48},{80,64},{96,80},{112,96},{128,112},... | collective-permute-start | bytes 1572872 | tf_op jit(solution)/shard_map/ppermute | solution.py:22
  50.1 174.0 %collective-permute-start = (f32[4,64,4,128]{3,2,1,0:T(4,128)}, f32[4,64,4,128]{3,2,1,0:T(4,128)}, u32[]{:S(2)}, u32[]{:S(2)}) collective-permute-start(f32[4,64,4,128]{3,2,1,0:T(4,128)} %get-tuple-element.20), channel_id=1, source_target_pairs={{0,16},{16,32},{32,48},{48,64},{64,80},{80,96},{96,112},{112,128},... | collective-permute-start | bytes 1572872 | tf_op jit(solution)/shard_map/ppermute | solution.py:19
  54.0 175.4 %copy-start.13 = (f32[3,64,8,128]{3,2,1,0:T(8,128)}, f32[3,64,8,128]{3,2,1,0:T(8,128)S(1)}, u32[]{:S(2)}) copy-start(f32[3,64,8,128]{3,2,1,0:T(8,128)S(1)} %convert_element_type.65) | copy-start | bytes 2359300
  125.4 5.1 collective-permute-start.5
  126.7 3.9 collective-permute-start.4
  132.1 29.7 %collective-permute-start.9 = (f32[1,4,8,128]{3,2,1,0:T(8,128)S(1)}, f32[1,4,8,128]{3,2,1,0:T(8,128)S(1)}, u32[]{:S(2)}, u32[]{:S(2)}) collective-permute-start(f32[1,4,8,128]{3,2,1,0:T(8,128)S(1)} %bitcast.138), channel_id=1, source_target_pairs={{1,0},{2,1},{3,2},{4,3},{5,4},{6,5},{7,6},{8,7},{9,8},{10,9},{11,1... | collective-permute-start | bytes 49160 | tf_op jit(solution)/shard_map/ppermute | solution.py:22
  159.8 8.3 %collective-permute-start.8 = (f32[1,4,8,128]{3,2,1,0:T(8,128)S(1)}, f32[1,4,8,128]{3,2,1,0:T(8,128)S(1)}, u32[]{:S(2)}, u32[]{:S(2)}) collective-permute-start(f32[1,4,8,128]{3,2,1,0:T(8,128)S(1)} %bitcast.139), channel_id=1, source_target_pairs={{0,1},{1,2},{2,3},{3,4},{4,5},{5,6},{6,7},{7,8},{8,9},{9,10},{10,1... | collective-permute-start | bytes 49160 | tf_op jit(solution)/shard_map/ppermute | solution.py:19
  168.1 48.6 %collective-permute-start.11 = (f32[1,12,4,128]{3,2,1,0:T(4,128)S(1)}, f32[1,12,4,128]{3,2,1,0:T(4,128)S(1)}, u32[]{:S(2)}, u32[]{:S(2)}) collective-permute-start(f32[1,12,4,128]{3,2,1,0:T(4,128)S(1)} %get-tuple-element.27), channel_id=1, source_target_pairs={{16,0},{32,16},{48,32},{64,48},{80,64},{96,80},{112,96},{128,112},... | collective-permute-start | bytes 73736 | tf_op jit(solution)/shard_map/ppermute | solution.py:22
  169.4 47.3 %collective-permute-start.10 = (f32[1,12,4,128]{3,2,1,0:T(4,128)S(1)}, f32[1,12,4,128]{3,2,1,0:T(4,128)S(1)}, u32[]{:S(2)}, u32[]{:S(2)}) collective-permute-start(f32[1,12,4,128]{3,2,1,0:T(4,128)S(1)} %get-tuple-element.26), channel_id=1, source_target_pairs={{0,16},{16,32},{32,48},{48,64},{64,80},{80,96},{96,112},{112,128},... | collective-permute-start | bytes 73736 | tf_op jit(solution)/shard_map/ppermute | solution.py:19
  218.3 26.6 %collective-permute-start.15 = (f32[1,4,8,128]{3,2,1,0:T(8,128)S(1)}, f32[1,4,8,128]{3,2,1,0:T(8,128)S(1)}, u32[]{:S(2)}, u32[]{:S(2)}) collective-permute-start(f32[1,4,8,128]{3,2,1,0:T(8,128)S(1)} %get-tuple-element.7), channel_id=1, source_target_pairs={{1,0},{2,1},{3,2},{4,3},{5,4},{6,5},{7,6},{8,7},{9,8},{10,9},{11,1... | collective-permute-start | bytes 49160 | tf_op jit(solution)/shard_map/ppermute | solution.py:22
  221.9 23.0 %collective-permute-start.14 = (f32[1,4,8,128]{3,2,1,0:T(8,128)S(1)}, f32[1,4,8,128]{3,2,1,0:T(8,128)S(1)}, u32[]{:S(2)}, u32[]{:S(2)}) collective-permute-start(f32[1,4,8,128]{3,2,1,0:T(8,128)S(1)} %get-tuple-element.7), channel_id=1, source_target_pairs={{0,1},{1,2},{2,3},{3,4},{4,5},{5,6},{6,7},{7,8},{8,9},{9,10},{10,1... | collective-permute-start | bytes 49160 | tf_op jit(solution)/shard_map/ppermute | solution.py:19
  240.2 65.2 %copy-start.6 = (bf16[4,64,8,128]{3,2,1,0:T(8,128)(2,1)S(1)}, bf16[4,64,8,128]{3,2,1,0:T(8,128)(2,1)}, u32[]{:S(2)}) copy-start(bf16[4,64,8,128]{3,2,1,0:T(8,128)(2,1)} %param.21) | copy-start | bytes 1572868
  240.2 65.2 %copy-start.7 = (f32[64,8,128]{2,1,0:T(8,128)S(1)}, f32[64,8,128]{2,1,0:T(8,128)}, u32[]{:S(2)}) copy-start(f32[64,8,128]{2,1,0:T(8,128)} %get-tuple-element.17) | copy-start | bytes 786436
  240.2 65.2 %copy-start.9 = (f32[64,8,128]{2,1,0:T(8,128)S(1)}, f32[64,8,128]{2,1,0:T(8,128)}, u32[]{:S(2)}) copy-start(f32[64,8,128]{2,1,0:T(8,128)} %get-tuple-element.18) | copy-start | bytes 786436
  240.4 62.3 %collective-permute-start.7 = (f32[4,64,4,128]{3,2,1,0:T(4,128)S(1)}, f32[4,64,4,128]{3,2,1,0:T(4,128)S(1)}, u32[]{:S(2)}, u32[]{:S(2)}) collective-permute-start(f32[4,64,4,128]{3,2,1,0:T(4,128)S(1)} %get-tuple-element.16), channel_id=1, source_target_pairs={{16,0},{32,16},{48,32},{64,48},{80,64},{96,80},{112,96},{128,112},... | collective-permute-start | bytes 1572872 | tf_op jit(solution)/shard_map/ppermute | solution.py:22
  241.9 60.9 %collective-permute-start.6 = (f32[4,64,4,128]{3,2,1,0:T(4,128)S(1)}, f32[4,64,4,128]{3,2,1,0:T(4,128)S(1)}, u32[]{:S(2)}, u32[]{:S(2)}) collective-permute-start(f32[4,64,4,128]{3,2,1,0:T(4,128)S(1)} %get-tuple-element.15), channel_id=1, source_target_pairs={{0,16},{16,32},{32,48},{48,64},{64,80},{80,96},{96,112},{112,128},... | collective-permute-start | bytes 1572872 | tf_op jit(solution)/shard_map/ppermute | solution.py:19
  245.0 57.7 %collective-permute-start.17 = (f32[1,12,4,128]{3,2,1,0:T(4,128)S(1)}, f32[1,12,4,128]{3,2,1,0:T(4,128)S(1)}, u32[]{:S(2)}, u32[]{:S(2)}) collective-permute-start(f32[1,12,4,128]{3,2,1,0:T(4,128)S(1)} %get-tuple-element.25), channel_id=1, source_target_pairs={{16,0},{32,16},{48,32},{64,48},{80,64},{96,80},{112,96},{128,112},... | collective-permute-start | bytes 73736 | tf_op jit(solution)/shard_map/ppermute | solution.py:22
  246.3 56.4 %collective-permute-start.16 = (f32[1,12,4,128]{3,2,1,0:T(4,128)S(1)}, f32[1,12,4,128]{3,2,1,0:T(4,128)S(1)}, u32[]{:S(2)}, u32[]{:S(2)}) collective-permute-start(f32[1,12,4,128]{3,2,1,0:T(4,128)S(1)} %get-tuple-element.24), channel_id=1, source_target_pairs={{0,16},{16,32},{32,48},{48,64},{64,80},{80,96},{96,112},{112,128},... | collective-permute-start | bytes 73736 | tf_op jit(solution)/shard_map/ppermute | solution.py:19
  311.8 63.4 %collective-permute-start.13 = (f32[4,64,4,128]{3,2,1,0:T(4,128)S(1)}, f32[4,64,4,128]{3,2,1,0:T(4,128)S(1)}, u32[]{:S(2)}, u32[]{:S(2)}) collective-permute-start(f32[4,64,4,128]{3,2,1,0:T(4,128)S(1)} %get-tuple-element.14), channel_id=1, source_target_pairs={{16,0},{32,16},{48,32},{64,48},{80,64},{96,80},{112,96},{128,112},... | collective-permute-start | bytes 1572872 | tf_op jit(solution)/shard_map/ppermute | solution.py:22
  313.1 62.1 %collective-permute-start.12 = (f32[4,64,4,128]{3,2,1,0:T(4,128)S(1)}, f32[4,64,4,128]{3,2,1,0:T(4,128)S(1)}, u32[]{:S(2)}, u32[]{:S(2)}) collective-permute-start(f32[4,64,4,128]{3,2,1,0:T(4,128)S(1)} %get-tuple-element.13), channel_id=1, source_target_pairs={{0,16},{16,32},{32,48},{48,64},{64,80},{80,96},{96,112},{112,128},... | collective-permute-start | bytes 1572872 | tf_op jit(solution)/shard_map/ppermute | solution.py:19
  318.4 52.3 %collective-permute-start.21 = (f32[1,4,8,128]{3,2,1,0:T(8,128)S(1)}, f32[1,4,8,128]{3,2,1,0:T(8,128)S(1)}, u32[]{:S(2)}, u32[]{:S(2)}) collective-permute-start(f32[1,4,8,128]{3,2,1,0:T(8,128)S(1)} %get-tuple-element.5), channel_id=1, source_target_pairs={{1,0},{2,1},{3,2},{4,3},{5,4},{6,5},{7,6},{8,7},{9,8},{10,9},{11,1... | collective-permute-start | bytes 49160 | tf_op jit(solution)/shard_map/ppermute | solution.py:22
  321.5 49.1 %collective-permute-start.20 = (f32[1,4,8,128]{3,2,1,0:T(8,128)S(1)}, f32[1,4,8,128]{3,2,1,0:T(8,128)S(1)}, u32[]{:S(2)}, u32[]{:S(2)}) collective-permute-start(f32[1,4,8,128]{3,2,1,0:T(8,128)S(1)} %get-tuple-element.5), channel_id=1, source_target_pairs={{0,1},{1,2},{2,3},{3,4},{4,5},{5,6},{6,7},{7,8},{8,9},{9,10},{10,1... | collective-permute-start | bytes 49160 | tf_op jit(solution)/shard_map/ppermute | solution.py:19
  370.7 28.1 %collective-permute-start.23 = (f32[1,12,4,128]{3,2,1,0:T(4,128)S(1)}, f32[1,12,4,128]{3,2,1,0:T(4,128)S(1)}, u32[]{:S(2)}, u32[]{:S(2)}) collective-permute-start(f32[1,12,4,128]{3,2,1,0:T(4,128)S(1)} %get-tuple-element.23), channel_id=1, source_target_pairs={{16,0},{32,16},{48,32},{64,48},{80,64},{96,80},{112,96},{128,112},... | collective-permute-start | bytes 73736 | tf_op jit(solution)/shard_map/ppermute | solution.py:22
  372.0 26.8 %collective-permute-start.22 = (f32[1,12,4,128]{3,2,1,0:T(4,128)S(1)}, f32[1,12,4,128]{3,2,1,0:T(4,128)S(1)}, u32[]{:S(2)}, u32[]{:S(2)}) collective-permute-start(f32[1,12,4,128]{3,2,1,0:T(4,128)S(1)} %get-tuple-element.22), channel_id=1, source_target_pairs={{0,16},{16,32},{32,48},{48,64},{64,80},{80,96},{96,112},{112,128},... | collective-permute-start | bytes 73736 | tf_op jit(solution)/shard_map/ppermute | solution.py:19
  386.1 145.5 %collective-permute-start.19 = (f32[4,64,4,128]{3,2,1,0:T(4,128)}, f32[4,64,4,128]{3,2,1,0:T(4,128)}, u32[]{:S(2)}, u32[]{:S(2)}) collective-permute-start(f32[4,64,4,128]{3,2,1,0:T(4,128)} %get-tuple-element.12), channel_id=1, source_target_pairs={{16,0},{32,16},{48,32},{64,48},{80,64},{96,80},{112,96},{128,112},... | collective-permute-start | bytes 1572872 | tf_op jit(solution)/shard_map/ppermute | solution.py:22
  387.4 144.2 %collective-permute-start.18 = (f32[4,64,4,128]{3,2,1,0:T(4,128)}, f32[4,64,4,128]{3,2,1,0:T(4,128)}, u32[]{:S(2)}, u32[]{:S(2)}) collective-permute-start(f32[4,64,4,128]{3,2,1,0:T(4,128)} %get-tuple-element.11), channel_id=1, source_target_pairs={{0,16},{16,32},{32,48},{48,64},{64,80},{80,96},{96,112},{112,128},... | collective-permute-start | bytes 1572872 | tf_op jit(solution)/shard_map/ppermute | solution.py:19
  543.9 86.7 %copy-start.1 = (bf16[4,32,32,128]{3,2,1,0:T(8,128)(2,1)S(1)}, bf16[4,32,32,128]{3,2,1,0:T(8,128)(2,1)}, u32[]{:S(2)}) copy-start(bf16[4,32,32,128]{3,2,1,0:T(8,128)(2,1)} %param.22) | copy-start | bytes 3145732
  (20 other events, 408.1 us)
